TPU v7x, 32 devices: a whole 2x2x4 slice. The times are simulated.
32 devices in a mesh: groups: 2 (over x), att: 8 (over z, y), exp: 2 (over core).
Axes of the slice: x: 2, y: 2, z: 4, core: 2. Of those that a mesh axis runs over, the one named last changes fastest.
Arguments:
- query: bfloat16 [2048, 2048], P(('groups', 'att'), 'exp'), parts along dimension 0, may hold values from -9 to 9
- new_key: bfloat16 [2048, 256], P(('groups', 'att'), 'exp'), parts along dimension 0, may hold values from -6 to 6
- new_value: bfloat16 [2048, 256], P(('groups', 'att'), 'exp'), parts along dimension 0, may hold values from -6 to 6
- cache_keys: bfloat16 [2048, 64, 256], P(('groups', 'att'), None, 'exp'), parts along dimension 0, may hold values from -9 to 9
- cache_values: bfloat16 [2048, 64, 256], P(('groups', 'att'), None, 'exp'), parts along dimension 0, may hold values from -6 to 6
- lengths: int32 [2048], P(('groups', 'att')), parts along dimension 0, may hold values from 2 to 64, as said below
- out_proj: bfloat16 [2048, 2880], P('exp'), may hold values from -0.125 to 0.125
- residual: bfloat16 [2048, 2880], P(('groups', 'att', 'exp')), parts along dimension 0, may hold values from -6 to 6
- norm_gain: float32 [2880], replicated, may hold values from 0.25 to 1.75
- router: float32 [2880, 8], replicated, may hold values from -0.21875 to 0.21875
- routes: int32 [2048, 4], P(('groups', 'att', 'exp')), parts along dimension 0, may hold values from 0 to 7, all different within a row; in each aligned block of 64 rows (0 to 63, 64 to 127, ...) at most 64 rows name the same one
- w_gate: bfloat16 [8, 2880, 1440], P('att', None, 'exp'), may hold values from -0.109375 to 0.109375
- w_up: bfloat16 [8, 2880, 1440], P('att', None, 'exp'), may hold values from -0.109375 to 0.109375
- w_down: bfloat16 [8, 1440, 2880], P('att', 'exp'), may hold values from -0.15625 to 0.15625
Outputs:
- mixed: bfloat16 [2048, 2880], P(('groups', 'att', 'exp')), parts along dimension 0
There are 2 independent parts, one for each index of `groups`. A program takes and returns all parts, laid end to end along the dimension named above; an argument that names none is the same for every part. Nothing has to cross between parts.
Inputs may be any that keep to these rules, and one draw needn't show every extreme that they name: `routes`: each row names 4 different experts. Among the 64 rows of one device (aligned blocks in order) no expert is named more than 64 times, and that count is reached in every draw. `lengths`: every eighth request, starting with the first, uses all 64 cached positions.
All inputs are finite; a program needn't handle non-finite values.
Results may differ from a plain program's by a relative error of at most 0.0065.
Values may be sent and summed in bfloat16 or wider, within the bound.
No kernel may reach another device: no remote copies, remote signals or barrier semaphores. Data moves between devices by JAX's collectives and lax.ppermute only.
A program may use at most 128 MiB of HBM per device.

v0:
```python
import math

import jax
import jax.numpy as jnp
from jax import lax
from jax.experimental import pallas as pl
from jax.experimental.pallas import tpu as pltpu
from jax.sharding import PartitionSpec as P

HEAD = 64
SUB = 8
STEP = 16
GRANT = 12 * 1024 * 1024
ACROSS = (((1,), (1,)), ((), ()))


def place_heads(queries, heads, slots, width):
    group_size = heads // slots
    slot_of_lane = lax.broadcasted_iota(jnp.int32, (SUB, width), 1) // HEAD
    pieces = []
    for head in range(heads):
        block, slot, home = head // slots, head % slots, head // group_size
        piece = queries[:, block * width : (block + 1) * width]
        if slot != home:
            piece = pltpu.roll(piece, ((home - slot) * HEAD) % width, 1)
        pieces.append(jnp.where(slot_of_lane == home, piece, 0.0))
    return jnp.concatenate(pieces, axis=0).astype(jnp.bfloat16)


def score(rows, keys, fresh_k, cache_len):
    request = lax.broadcasted_iota(jnp.int32, (cache_len, rows.shape[0]), 1) % SUB
    spread = lax.dot_general(keys, rows, ACROSS, preferred_element_type=jnp.float32)
    scores = spread[:cache_len]
    for r in range(1, SUB):
        scores = jnp.where(request == r, spread[r * cache_len : (r + 1) * cache_len], scores)
    return scores, lax.dot_general(fresh_k, rows, ACROSS, preferred_element_type=jnp.float32)


def soften(scores, fresh, live, offset, per):
    cache_len, count = scores.shape
    request = lax.broadcasted_iota(jnp.int32, (cache_len, count), 1) % SUB
    place = lax.broadcasted_iota(jnp.int32, (cache_len, count), 0)
    scores = jnp.where(place < live, scores, -1e30)
    fresh_place = lax.broadcasted_iota(jnp.int32, fresh.shape, 0)
    fresh_own = fresh_place == offset + lax.broadcasted_iota(jnp.int32, fresh.shape, 1) % SUB
    fresh_scores = jnp.sum(jnp.where(fresh_own, fresh, 0.0), axis=0, keepdims=True)
    highest = jnp.maximum(jnp.max(scores, axis=0, keepdims=True), fresh_scores)
    cached_exp = jnp.exp(scores - highest)
    fresh_exp = jnp.exp(fresh_scores - highest)
    scale = 1.0 / (jnp.sum(cached_exp, axis=0, keepdims=True) + fresh_exp)
    probs = cached_exp * scale
    fresh_probs = jnp.where(fresh_own, fresh_exp * scale, 0.0)
    return jnp.concatenate(
        [jnp.where(request % per == i, probs, 0.0) for i in range(per)] + [fresh_probs], axis=0
    ).T


def weigh(turned, values, fresh_v, per):
    count, width = turned.shape[0], values.shape[1]
    group = lax.broadcasted_iota(jnp.int32, (count, width), 0) % SUB // per
    wide = jnp.concatenate(
        [jnp.where(group == part, turned[:, :width], 0.0) for part in range(SUB // per)], axis=1
    ).astype(jnp.bfloat16)
    output = jnp.dot(wide, values, preferred_element_type=jnp.float32)
    return output + jnp.dot(
        turned[:, width:].astype(jnp.bfloat16), fresh_v, preferred_element_type=jnp.float32
    )


def gather_heads(output, heads, slots, width):
    group_size = heads // slots
    slot_of_lane = lax.broadcasted_iota(jnp.int32, (SUB, width), 1) // HEAD
    blocks = []
    for block in range(heads // slots):
        merged = None
        for slot in range(slots):
            head = block * slots + slot
            home = head // group_size
            piece = output[head * SUB : (head + 1) * SUB]
            if slot != home:
                piece = pltpu.roll(piece, ((slot - home) * HEAD) % width, 1)
            merged = piece if merged is None else jnp.where(slot_of_lane == slot, piece, merged)
        blocks.append(merged)
    return jnp.concatenate(blocks, axis=-1)


def attend(first, lengths_ref, q_ref, nk_ref, nv_ref, k_ref, v_ref, att_ref, ready):
    width = nk_ref.shape[1]
    slots = width // HEAD
    heads = q_ref.shape[1] // HEAD
    cache_len = k_ref.shape[1]
    per = width // cache_len
    request = lax.broadcasted_iota(jnp.int32, (1, heads * SUB), 1) % SUB
    batches = range(0, att_ref.shape[0], SUB)
    scores = []
    for at in batches:
        step = at // STEP * STEP
        if at == step:
            ready(at)
            queries = q_ref[step : step + STEP].astype(jnp.float32) * (1.0 / math.sqrt(HEAD))
        rows = place_heads(queries[at - step : at - step + SUB], heads, slots, width)
        keys = k_ref[at : at + SUB].reshape(SUB * cache_len, width)
        scores.append(score(rows, keys, nk_ref[step : step + STEP], cache_len))
    turned = []
    for at, (cached, fresh) in zip(batches, scores):
        live = jnp.zeros(request.shape, jnp.int32)
        for i in range(SUB):
            live = jnp.where(request == i, lengths_ref[first + at + i], live)
        turned.append(soften(cached, fresh, live, at % STEP, per))
    outputs = []
    for at, probs in zip(batches, turned):
        step = at // STEP * STEP
        values = v_ref[at : at + SUB].reshape(SUB * cache_len, width)
        outputs.append(weigh(probs, values, nv_ref[step : step + STEP], per))
    for step in range(0, att_ref.shape[0], STEP):
        pair = outputs[step // SUB : (step + STEP) // SUB]
        att_ref[step : step + STEP, :] = jnp.concatenate(
            [gather_heads(output, heads, slots, width) for output in pair], axis=0
        ).astype(jnp.bfloat16)


def project(att_ref, w_ref, out_ref):
    turned = lax.dot_general(
        w_ref[...], att_ref[...], ACROSS, preferred_element_type=jnp.float32
    )
    out_ref[...] = turned.T


def first_kernel(
    core_ref, chip_ref, lengths_hbm, q_hbm, nk_hbm, nv_hbm, k_hbm, v_hbm, w_hbm,
    out_ref, w_ref, own_k, own_v, lengths_ref, q_ref, nk_ref, nv_ref, k_ref, v_ref, att_ref, sems,
):
    rows = out_ref.shape[0]
    theirs = pl.multiple_of((1 - core_ref[0]) * rows, rows)
    mine = pl.multiple_of(core_ref[0] * rows, rows)
    copies = []

    def bring(source, target):
        copy = pltpu.make_async_copy(source, target, sems.at[len(copies)])
        copy.start()
        copies.append(copy)
        return copy

    small = [bring(lengths_hbm, lengths_ref)] + [
        bring(source.at[pl.ds(theirs, rows)], target)
        for source, target in ((q_hbm, q_ref), (nk_hbm, nk_ref), (nv_hbm, nv_ref))
    ]
    cache = []
    for at in range(0, rows, STEP):
        span = pl.ds(theirs + at, STEP)
        cache.append(
            (
                bring(k_hbm.at[span], k_ref.at[pl.ds(at, STEP)]),
                bring(v_hbm.at[span], v_ref.at[pl.ds(at, STEP)]),
            )
        )
    pieces = 4
    columns = w_ref.shape[0]
    size = -(-columns // pieces // 16) * 16
    weights = []
    for at in range(0, columns, size):
        span = pl.ds(at, min(size, columns - at))
        weights.append(bring(w_hbm.at[span], w_ref.at[span]))
    later = [
        bring(k_hbm.at[pl.ds(mine, rows)], own_k),
        bring(v_hbm.at[pl.ds(mine, rows)], own_v),
    ]
    for copy in small:
        copy.wait()

    def ready(at):
        for copy in cache[at // STEP]:
            copy.wait()

    attend(theirs, lengths_ref, q_ref, nk_ref, nv_ref, k_ref, v_ref, att_ref, ready)
    for copy in weights:
        copy.wait()
    project(att_ref, w_ref, out_ref)
    for copy in later:
        copy.wait()


def second_kernel(
    core_ref, lengths_ref, q_ref, nk_ref, nv_ref, k_ref, v_ref, w_ref, out_ref, att_ref
):
    rows = out_ref.shape[0]
    mine = pl.multiple_of(core_ref[0] * rows, rows)
    own = [ref.at[pl.ds(mine, rows)] for ref in (q_ref, nk_ref, nv_ref)]
    attend(mine, lengths_ref, *own, k_ref, v_ref, att_ref, lambda at: None)
    project(att_ref, w_ref, out_ref)


def attend_theirs(
    core, rows, lengths, query, new_key, new_value, cache_keys, cache_values, w, chip
):
    cache = (rows,) + cache_keys.shape[1:]
    columns = w.shape[0]
    smem = pl.BlockSpec(memory_space=pltpu.SMEM)
    vmem = pl.BlockSpec(memory_space=pltpu.VMEM)
    hbm = pl.BlockSpec(memory_space=pltpu.HBM)
    copies = 4 + 2 * (rows // STEP) + 4 + 2
    return pl.pallas_call(
        first_kernel,
        out_shape=(
            jax.ShapeDtypeStruct((rows, columns), jnp.float32),
            jax.ShapeDtypeStruct(w.shape, jnp.bfloat16),
            jax.ShapeDtypeStruct(cache, jnp.bfloat16),
            jax.ShapeDtypeStruct(cache, jnp.bfloat16),
        ),
        in_specs=[smem] * 2 + [hbm] * 7,
        out_specs=[vmem] * 4,
        scratch_shapes=[
            pltpu.SMEM(lengths.shape, jnp.int32),
            pltpu.VMEM((rows, query.shape[1]), jnp.bfloat16),
            pltpu.VMEM((rows, new_key.shape[1]), jnp.bfloat16),
            pltpu.VMEM((rows, new_key.shape[1]), jnp.bfloat16),
            pltpu.VMEM(cache, jnp.bfloat16),
            pltpu.VMEM(cache, jnp.bfloat16),
            pltpu.VMEM((rows, query.shape[1]), jnp.bfloat16),
            pltpu.SemaphoreType.DMA((copies,)),
        ],
        compiler_params=pltpu.CompilerParams(vmem_limit_bytes=GRANT),
        cost_estimate=pl.CostEstimate(
            flops=2 * rows * w.size, bytes_accessed=2 * w.size, transcendentals=0
        ),
    )(
        core,
        chip,
        *(
            pltpu.with_memory_space_constraint(x, pltpu.HBM)
            for x in (lengths, query, new_key, new_value, cache_keys, cache_values, w)
        ),
    )


def attend_mine(core, rows, lengths, query, new_key, new_value, own_keys, own_values, w):
    smem = pl.BlockSpec(memory_space=pltpu.SMEM)
    vmem = pl.BlockSpec(memory_space=pltpu.VMEM)
    return pl.pallas_call(
        second_kernel,
        out_shape=jax.ShapeDtypeStruct((rows, w.shape[0]), jnp.float32),
        in_specs=[smem, smem] + [vmem] * 6,
        out_specs=vmem,
        scratch_shapes=[pltpu.VMEM((rows, query.shape[1]), jnp.bfloat16)],
        compiler_params=pltpu.CompilerParams(vmem_limit_bytes=GRANT),
        cost_estimate=pl.CostEstimate(
            flops=2 * rows * w.size, bytes_accessed=2 * w.size, transcendentals=0
        ),
    )(core, lengths, query, new_key, new_value, own_keys, own_values, w)


def norm_kernel(
    mine_ref, swapped_ref, residual_ref, gain_ref, router_ref, routes_ref, hidden_ref, payload_ref
):
    hidden = residual_ref[...].astype(jnp.float32) + (mine_ref[...] + swapped_ref[...])
    hidden_ref[...] = hidden
    rows, width = hidden.shape
    mean_square = jnp.sum(hidden * hidden, axis=-1, keepdims=True) * (1.0 / width)
    normed = (hidden * lax.rsqrt(mean_square + 1e-05) * gain_ref[...]).astype(jnp.bfloat16)
    payload_ref[:, :width] = normed
    rest = router_ref[...]
    experts = rest.shape[0]
    terms = []
    for _ in range(3):
        term = rest.astype(jnp.bfloat16).astype(jnp.float32)
        terms.append(term)
        rest = rest - term
    parts = lax.dot_general(
        jnp.concatenate(terms, axis=0).astype(jnp.bfloat16),
        normed,
        (((1,), (1,)), ((), ())),
        preferred_element_type=jnp.float32,
    )
    logits = parts[:experts] + parts[experts : 2 * experts] + parts[2 * experts :]
    number = lax.broadcasted_iota(jnp.int32, (experts, rows), 0)
    chosen = number == routes_ref[0:1, :]
    for k in range(1, routes_ref.shape[0]):
        chosen = chosen | (number == routes_ref[k : k + 1, :])
    squashed = jnp.where(chosen, 1.0 / (1.0 + jnp.exp(-logits)), 0.0)
    gates = squashed / jnp.sum(squashed, axis=0, keepdims=True)
    upper = gates.astype(jnp.bfloat16).astype(jnp.float32)
    both = jnp.concatenate([upper, gates - upper], axis=0).astype(jnp.bfloat16)
    tail = payload_ref.shape[1] - width
    place = lax.broadcasted_iota(jnp.int32, (2 * experts, tail), 0)
    lane = lax.broadcasted_iota(jnp.int32, (2 * experts, tail), 1)
    placed = lax.dot_general(
        both,
        (place == lane).astype(jnp.bfloat16),
        (((0,), (0,)), ((), ())),
        preferred_element_type=jnp.float32,
    )
    payload_ref[:, width:] = placed.astype(jnp.bfloat16)


def norm_route(mine, swapped, residual, norm_gain, router, routes):
    rows, width = residual.shape
    experts = router.shape[1]
    wide = -(-(width + 2 * experts) // 128) * 128
    return pl.pallas_call(
        norm_kernel,
        out_shape=(
            jax.ShapeDtypeStruct((rows, width), jnp.float32),
            jax.ShapeDtypeStruct((rows, wide), jnp.bfloat16),
        ),
        compiler_params=pltpu.CompilerParams(vmem_limit_bytes=GRANT),
    )(mine, swapped, residual, norm_gain[None, :], router.T, routes.T)


def expert_kernel(count, experts, chip_ref, *refs):
    blocks, refs = refs[:count], refs[count:]
    gate_ref, up_ref, down_ref = refs[:3]
    outs, act_ref = refs[3:-1], refs[-1]
    _, hidden, width = gate_ref.shape
    rows = jnp.concatenate([block[...] for block in blocks], axis=0)
    base = width // 128 * 128
    tail = rows[:, base:].astype(jnp.float32)
    lane = lax.broadcasted_iota(jnp.int32, tail.shape, 1) - (width - base)
    named = (lane == chip_ref[0]) | (lane == chip_ref[0] + experts)
    weight = jnp.sum(jnp.where(named, tail, 0.0), axis=-1, keepdims=True)
    turned = rows[:, :width].T
    gate = jnp.dot(gate_ref[0], turned, preferred_element_type=jnp.float32)
    up = jnp.dot(up_ref[0], turned, preferred_element_type=jnp.float32)
    act_ref[...] = (gate / (1.0 + jnp.exp(-gate)) * up).T.astype(jnp.bfloat16)
    for at in range(0, width, 768):
        span = slice(at, min(at + 768, width))
        part = jnp.dot(act_ref[...], down_ref[0, :, span], preferred_element_type=jnp.float32)
        part = (part * weight).astype(jnp.bfloat16)
        first = 0
        for out in outs:
            out[:, span] = part[first : first + out.shape[0]]
            first += out.shape[0]


def run_expert(chip, blocks, gate_t, up_t, down, experts, cost):
    _, hidden, width = down.shape
    rows = sum(block.shape[0] for block in blocks)
    count = len(blocks)
    vmem = pl.BlockSpec(memory_space=pltpu.VMEM)
    return pl.pallas_call(
        lambda *refs: expert_kernel(count, experts, *refs),
        out_shape=[jax.ShapeDtypeStruct((b.shape[0], width), jnp.bfloat16) for b in blocks],
        in_specs=[pl.BlockSpec(memory_space=pltpu.SMEM)] + [vmem] * (count + 3),
        out_specs=[vmem] * count,
        scratch_shapes=[pltpu.VMEM((rows, hidden), jnp.bfloat16)],
        compiler_params=pltpu.CompilerParams(vmem_limit_bytes=GRANT),
        cost_estimate=pl.CostEstimate(
            flops=6 * cost * rows * hidden * width,
            bytes_accessed=6 * cost * hidden * width,
            transcendentals=0,
        ),
    )(chip, *blocks, gate_t, up_t, down)


def add_kernel(firsts, *refs):
    size = refs[-1].shape[0]
    total = None
    for first, ref in zip(firsts, refs):
        term = ref[first : first + size].astype(jnp.float32)
        total = term if total is None else total + term
    refs[-1][...] = total.astype(refs[-1].dtype)


def add_rows(size, *parts, dtype=jnp.bfloat16):
    firsts = [first for _, first in parts]
    width = parts[0][0].shape[1]
    return pl.pallas_call(
        lambda *refs: add_kernel(firsts, *refs),
        out_shape=jax.ShapeDtypeStruct((size, width), dtype),
        compiler_params=pltpu.CompilerParams(vmem_limit_bytes=GRANT),
    )(*[array for array, _ in parts])


def add_all(*terms, dtype=jnp.bfloat16):
    return add_rows(terms[0].shape[0], *[(term, 0) for term in terms], dtype=dtype)


def finish_kernel(*refs):
    *whole, top, low, top_y, low_y, out = refs
    first = 0
    for half, half_y in ((top, top_y), (low, low_y)):
        size = half.shape[0]
        total = half[...].astype(jnp.float32) + half_y[...].astype(jnp.float32)
        for ref in whole:
            total = total + ref[first : first + size].astype(jnp.float32)
        out[first : first + size, :] = total.astype(out.dtype)
        first += size


def finish(*arrays):
    return pl.pallas_call(
        finish_kernel,
        out_shape=jax.ShapeDtypeStruct(arrays[0].shape, jnp.bfloat16),
        compiler_params=pltpu.CompilerParams(vmem_limit_bytes=GRANT),
    )(*arrays)


def ring_pairs(chips, cores, cross):
    order = list(range(0, chips, 2)) + list(range(1, chips, 2))[::-1]
    pairs = []
    for p in range(chips):
        for core in range(cores):
            turn = -1 if core % 2 else 1
            to = core ^ 1 if cross else core
            pairs.append((order[p] * cores + core, order[(p + turn) % chips] * cores + to))
    return pairs


def per_device(
    query,
    new_key,
    new_value,
    cache_keys,
    cache_values,
    lengths,
    out_proj,
    residual,
    norm_gain,
    router,
    routes,
    w_gate,
    w_up,
    w_down,
):
    chips, cores = lax.axis_size("att"), lax.axis_size("exp")
    own_rows = residual.shape[0]
    ring = ("att", "exp")

    def send(x, cross=False):
        return lax.ppermute(x, ring, ring_pairs(chips, cores, cross))

    def swap(x):
        return lax.ppermute(x, "exp", [(0, 1), (1, 0)])

    core = jnp.full((1,), lax.axis_index("exp"), jnp.int32)
    chip = jnp.full((1,), lax.axis_index("att"), jnp.int32)
    small = (core, own_rows, lengths, query, new_key, new_value)
    theirs, w_out, own_keys, own_values = attend_theirs(
        *small, cache_keys, cache_values, out_proj.T, chip
    )
    swapped = swap(theirs)
    mine = attend_mine(*small, own_keys, own_values, w_out)
    hidden_state, payload = norm_route(mine, swapped, residual, norm_gain, router, routes)

    experts = router.shape[1]

    far = chips // 2

    def after(value, *earlier):
        return lax.optimization_barrier((value, earlier))[0]

    gate_t, up_t = w_gate.transpose(0, 2, 1), w_up.transpose(0, 2, 1)

    def expert(blocks, cost=5):
        return run_expert(chip, blocks, gate_t, up_t, w_down, experts, cost)

    x, y = payload, swap(payload)
    done = expert((x, y), cost=1)
    own, own_other = done[0], swap(done[1])
    sums_x, sums_y = [None], [None]
    swapped_y = None
    for k in range(1, far + 1):
        x = send(x)
        if k in (1, far):
            x = after(x, done[0])
        blocks = [x, swap(x)]
        if k > 1:
            blocks += swapped_y
        if k < far:
            y = send(y)
            if k > 1:
                y = after(y, done[0])
            swapped_y = [y, swap(y)]
        if 2 < k < far:
            blocks[1] = after(blocks[1], sums_x[k - 2][1], *([sums_y[k - 2][1]] if k > 3 else []))
        done = expert(blocks)
        sums_x.append((done[1], swap(done[0])))
        if k > 1:
            sums_y.append((done[3], swap(done[2])))

    held = add_all(hidden_state, own, own_other, dtype=jnp.float32)
    middle = own_rows // 2
    back_x, back_y = [[], []], [[], []]
    for k in range(far, 0, -1):
        for half in (0, 1):
            mine_x = [(term, half * middle) for term in sums_x[k]] + back_x[half]
            back_x[half] = [(send(add_rows(middle, *mine_x), k == 1), 0)]
            if k < far:
                mine_y = [(term, half * middle) for term in sums_y[k]] + back_y[half]
                back_y[half] = [(send(add_rows(middle, *mine_y)), 0)]
    return finish(held, *[half[0][0] for half in back_x + back_y])


def solution(mesh):
    in_specs = (
        P(("groups", "att"), "exp"),
        P(("groups", "att"), "exp"),
        P(("groups", "att"), "exp"),
        P(("groups", "att"), None, "exp"),
        P(("groups", "att"), None, "exp"),
        P(("groups", "att")),
        P("exp", None),
        P(("groups", "att", "exp"), None),
        P(),
        P(),
        P(("groups", "att", "exp"), None),
        P("att", None, "exp"),
        P("att", None, "exp"),
        P("att", "exp", None),
    )
    out_specs = P(("groups", "att", "exp"), None)
    return jax.shard_map(
        per_device, mesh=mesh, in_specs=in_specs, out_specs=out_specs, check_vma=False
    )
```

profile of v0, /device:TPU:0, one launch (start us, length us, event | category | flops | bytes accessed | tf_op | source)
XLA Modules:
  0.0 84.7 jit_solution(2164010443498853295)
XLA Ops:
  0.0 5.5 %shard_map.136 = (f32[64,2880]{1,0:T(8,128)S(1)}, bf16[2880,1024]{1,0:T(8,128)(2,1)S(1)}, bf16[64,64,128]{2,1,0:T(8,128)(2,1)S(1)}, bf16[64,64,128]{2,1,0:T(8,128)(2,1)S(1)}) custom-call(s32[1]{0:T(128)} %bitcast.core_ref, s32[1]{0:T(128)} %bitcast.1.chip_ref.refs_0_, s32[128]{0:T(128)} %lengths_ref.1, bf16[128,1024]{1,0:T(8,128)(2,1)} %q_ref.1, ...), custom_call_target="tpu_custom_call" | custom-call | flops 377487360 | bytes 5898240 | tf_op jit(solution)/shard_map/pallas_call | solution.py:202
  6.2 3.4 %shard_map.137.mine_ref = f32[64,2880]{1,0:T(8,128)S(1)} custom-call(s32[1]{0:T(128)} %bitcast.core_ref, s32[128]{0:T(128)S(1)} %copy-done.7, bf16[128,1024]{1,0:T(8,128)(2,1)S(1)} %copy-done.2, bf16[128,128]{1,0:T(8,128)(2,1)S(1)} %copy-done.4, bf16[128,128]{1,0:T(8,128)(2,1)S(1)} %copy-done.5, bf16[64,64,128]{2,1,0:T(8,128)(2,1)S(1)} %get-tuple-element.32.k_ref, ...), custom_call_target="tpu_custom_call" | custom-call | flops 377487360 | bytes 5898240 | tf_op jit(solution)/shard_map/pallas_call | solution.py:239
  10.4 3.0 %collective-permute-start.3 = (bf16[64,2944]{1,0:T(8,128)(2,1)S(1)}, bf16[64,2944]{1,0:T(8,128)(2,1)S(1)}, u32[]{:S(2)}, u32[]{:S(2)}) collective-permute-start(bf16[64,2944]{1,0:T(8,128)(2,1)S(1)} %get-tuple-element.37.refs_1_), channel_id=1, source_target_pairs={{0,4},{1,3},{4,8},{5,1},{8,12},{9,5},{12,14},{13,9},{14,10},{15,13... | collective-permute-start | bytes 1130504 | tf_op jit(solution)/shard_map/ppermute | solution.py:429
  13.5 1.6 %collective-permute-start.8 = (bf16[64,2944]{1,0:T(8,128)(2,1)S(1)}, bf16[64,2944]{1,0:T(8,128)(2,1)S(1)}, u32[]{:S(2)}, u32[]{:S(2)}) collective-permute-start(bf16[64,2944]{1,0:T(8,128)(2,1)S(1)} %collective-permute-done.1.refs_2_), channel_id=1, source_target_pairs={{0,4},{1,3},{4,8},{5,1},{8,12},{9,5},{12,14},{13,9},{14,10},{15,13... | collective-permute-start | bytes 1130504 | tf_op jit(solution)/shard_map/ppermute | solution.py:429
  15.1 3.2 %shard_map.139 = (bf16[64,2880]{1,0:T(8,128)(2,1)S(1)}, bf16[64,2880]{1,0:T(8,128)(2,1)S(1)}) custom-call(s32[1]{0:T(128)} %bitcast.1.chip_ref.refs_0_, bf16[64,2944]{1,0:T(8,128)(2,1)S(1)} %get-tuple-element.37.refs_1_, bf16[64,2944]{1,0:T(8,128)(2,1)S(1)} %collective-permute-done.1.refs_2_, bf16[1,720,2880]{2,1,0:T(8,128)(2,1)S(1)} %bitcast.9, ...), custom_call_target="tpu_custom_call" | custom-call | flops 1592524800 | bytes 12441600 | tf_op jit(solution)/shard_map/pallas_call | solution.py:339
  19.0 2.1 %collective-permute-start.6 = (bf16[64,2944]{1,0:T(8,128)(2,1)S(1)}, bf16[64,2944]{1,0:T(8,128)(2,1)S(1)}, u32[]{:S(2)}, u32[]{:S(2)}) collective-permute-start(bf16[64,2944]{1,0:T(8,128)(2,1)S(1)} %collective-permute-done.3.refs_1_), channel_id=1, source_target_pairs={{0,4},{1,3},{4,8},{5,1},{8,12},{9,5},{12,14},{13,9},{14,10},{15,13... | collective-permute-start | bytes 1130504 | tf_op jit(solution)/shard_map/ppermute | solution.py:429
  21.1 2.0 %collective-permute-done.8.refs_3_ = bf16[64,2944]{1,0:T(8,128)(2,1)S(1)} collective-permute-done((bf16[64,2944]{1,0:T(8,128)(2,1)S(1)}, bf16[64,2944]{1,0:T(8,128)(2,1)S(1)}, u32[]{:S(2)}, u32[]{:S(2)}) %collective-permute-start.8) | collective-permute-done | bytes 376864 | tf_op jit(solution)/shard_map/ppermute | solution.py:429
  23.0 2.1 %collective-permute-start.13 = (bf16[64,2944]{1,0:T(8,128)(2,1)S(1)}, bf16[64,2944]{1,0:T(8,128)(2,1)S(1)}, u32[]{:S(2)}, u32[]{:S(2)}) collective-permute-start(bf16[64,2944]{1,0:T(8,128)(2,1)S(1)} %collective-permute-done.8.refs_3_), channel_id=1, source_target_pairs={{0,4},{1,3},{4,8},{5,1},{8,12},{9,5},{12,14},{13,9},{14,10},{15,13... | collective-permute-start | bytes 1130504 | tf_op jit(solution)/shard_map/ppermute | solution.py:429
  25.1 2.0 %collective-permute-done.6.refs_1_ = bf16[64,2944]{1,0:T(8,128)(2,1)S(1)} collective-permute-done((bf16[64,2944]{1,0:T(8,128)(2,1)S(1)}, bf16[64,2944]{1,0:T(8,128)(2,1)S(1)}, u32[]{:S(2)}, u32[]{:S(2)}) %collective-permute-start.6) | collective-permute-done | bytes 376864 | tf_op jit(solution)/shard_map/ppermute | solution.py:429
  27.1 2.1 %collective-permute-start.11 = (bf16[64,2944]{1,0:T(8,128)(2,1)S(1)}, bf16[64,2944]{1,0:T(8,128)(2,1)S(1)}, u32[]{:S(2)}, u32[]{:S(2)}) collective-permute-start(bf16[64,2944]{1,0:T(8,128)(2,1)S(1)} %collective-permute-done.6.refs_1_), channel_id=1, source_target_pairs={{0,4},{1,3},{4,8},{5,1},{8,12},{9,5},{12,14},{13,9},{14,10},{15,13... | collective-permute-start | bytes 1130504 | tf_op jit(solution)/shard_map/ppermute | solution.py:429
  29.1 3.2 %shard_map.141 = (bf16[64,2880]{1,0:T(8,128)(2,1)S(1)}, bf16[64,2880]{1,0:T(8,128)(2,1)S(1)}) custom-call(s32[1]{0:T(128)} %bitcast.1.chip_ref.refs_0_, bf16[64,2944]{1,0:T(8,128)(2,1)S(1)} %collective-permute-done.3.refs_1_, bf16[64,2944]{1,0:T(8,128)(2,1)S(1)} %collective-permute-done.4.refs_2_, bf16[1,720,2880]{2,1,0:T(8,128)(2,1)S(1)} %bitcast.10, ...), custom_call_target="tpu_custom_call" | custom-call | flops 7962624000 | bytes 62208000 | tf_op jit(solution)/shard_map/pallas_call | solution.py:339
  35.1 2.1 %collective-permute-start.16 = (bf16[64,2944]{1,0:T(8,128)(2,1)S(1)}, bf16[64,2944]{1,0:T(8,128)(2,1)S(1)}, u32[]{:S(2)}, u32[]{:S(2)}) collective-permute-start(bf16[64,2944]{1,0:T(8,128)(2,1)S(1)} %collective-permute-done.11.refs_1_), channel_id=1, source_target_pairs={{0,4},{1,3},{4,8},{5,1},{8,12},{9,5},{12,14},{13,9},{14,10},{15,13... | collective-permute-start | bytes 1130504 | tf_op jit(solution)/shard_map/ppermute | solution.py:429
  37.2 3.8 %shard_map.142 = (bf16[64,2880]{1,0:T(8,128)(2,1)S(1)}, bf16[64,2880]{1,0:T(8,128)(2,1)S(1)}, bf16[64,2880]{1,0:T(8,128)(2,1)S(1)}, bf16[64,2880]{1,0:T(8,128)(2,1)S(1)}) custom-call(s32[1]{0:T(128)} %bitcast.1.chip_ref.refs_0_, bf16[64,2944]{1,0:T(8,128)(2,1)S(1)} %collective-permute-done.6.refs_1_, bf16[64,2944]{1,0:T(8,128)(2,1)S(1)} %collective-permute-done.7.refs_2_, ...), custom_call_target="tpu_custom_call" | custom-call | flops 15925248000 | bytes 62208000 | tf_op jit(solution)/shard_map/pallas_call | solution.py:339
  41.3 3.8 %shard_map.143 = (bf16[64,2880]{1,0:T(8,128)(2,1)S(1)}, bf16[64,2880]{1,0:T(8,128)(2,1)S(1)}, bf16[64,2880]{1,0:T(8,128)(2,1)S(1)}, bf16[64,2880]{1,0:T(8,128)(2,1)S(1)}) custom-call(s32[1]{0:T(128)} %bitcast.1.chip_ref.refs_0_, bf16[64,2944]{1,0:T(8,128)(2,1)S(1)} %collective-permute-done.11.refs_1_, bf16[64,2944]{1,0:T(8,128)(2,1)S(1)} %collective-permute-done.12.refs_2_, ...), custom_call_target="tpu_custom_call" | custom-call | flops 15925248000 | bytes 62208000 | tf_op jit(solution)/shard_map/pallas_call | solution.py:339
  47.0 3.8 %shard_map.144 = (bf16[64,2880]{1,0:T(8,128)(2,1)S(1)}, bf16[64,2880]{1,0:T(8,128)(2,1)S(1)}, bf16[64,2880]{1,0:T(8,128)(2,1)S(1)}, bf16[64,2880]{1,0:T(8,128)(2,1)S(1)}) custom-call(s32[1]{0:T(128)} %bitcast.1.chip_ref.refs_0_, bf16[64,2944]{1,0:T(8,128)(2,1)S(1)} %collective-permute-done.16.refs_1_, bf16[64,2944]{1,0:T(8,128)(2,1)S(1)} %collective-permute-done.17.refs_2_, ...), custom_call_target="tpu_custom_call" | custom-call | flops 15925248000 | bytes 62208000 | tf_op jit(solution)/shard_map/pallas_call | solution.py:339
  52.6 1.6 %collective-permute-start.25 = (bf16[32,2880]{1,0:T(8,128)(2,1)S(1)}, bf16[32,2880]{1,0:T(8,128)(2,1)S(1)}, u32[]{:S(2)}, u32[]{:S(2)}) collective-permute-start(bf16[32,2880]{1,0:T(8,128)(2,1)S(1)} %shard_map.149), channel_id=1, source_target_pairs={{0,4},{1,3},{4,8},{5,1},{8,12},{9,5},{12,14},{13,9},{14,10},{15,13... | collective-permute-start | bytes 552968 | tf_op jit(solution)/shard_map/ppermute | solution.py:429
  54.3 1.6 %collective-permute-start.21 = (bf16[32,2880]{1,0:T(8,128)(2,1)S(1)}, bf16[32,2880]{1,0:T(8,128)(2,1)S(1)}, u32[]{:S(2)}, u32[]{:S(2)}) collective-permute-start(bf16[32,2880]{1,0:T(8,128)(2,1)S(1)} %shard_map.145), channel_id=1, source_target_pairs={{0,4},{1,3},{4,8},{5,1},{8,12},{9,5},{12,14},{13,9},{14,10},{15,13... | collective-permute-start | bytes 552968 | tf_op jit(solution)/shard_map/ppermute | solution.py:429
  56.0 1.6 %collective-permute-start.35 = (bf16[32,2880]{1,0:T(8,128)(2,1)S(1)}, bf16[32,2880]{1,0:T(8,128)(2,1)S(1)}, u32[]{:S(2)}, u32[]{:S(2)}) collective-permute-start(bf16[32,2880]{1,0:T(8,128)(2,1)S(1)} %shard_map.156), channel_id=1, source_target_pairs={{0,4},{1,3},{4,8},{5,1},{8,12},{9,5},{12,14},{13,9},{14,10},{15,13... | collective-permute-start | bytes 552968 | tf_op jit(solution)/shard_map/ppermute | solution.py:429
  60.3 1.6 %collective-permute-start.26 = (bf16[32,2880]{1,0:T(8,128)(2,1)S(1)}, bf16[32,2880]{1,0:T(8,128)(2,1)S(1)}, u32[]{:S(2)}, u32[]{:S(2)}) collective-permute-start(bf16[32,2880]{1,0:T(8,128)(2,1)S(1)} %shard_map.150), channel_id=1, source_target_pairs={{0,4},{1,3},{4,8},{5,1},{8,12},{9,5},{12,14},{13,9},{14,10},{15,13... | collective-permute-start | bytes 552968 | tf_op jit(solution)/shard_map/ppermute | solution.py:429
  62.3 1.6 %collective-permute-start.22 = (bf16[32,2880]{1,0:T(8,128)(2,1)S(1)}, bf16[32,2880]{1,0:T(8,128)(2,1)S(1)}, u32[]{:S(2)}, u32[]{:S(2)}) collective-permute-start(bf16[32,2880]{1,0:T(8,128)(2,1)S(1)} %shard_map.146), channel_id=1, source_target_pairs={{0,4},{1,3},{4,8},{5,1},{8,12},{9,5},{12,14},{13,9},{14,10},{15,13... | collective-permute-start | bytes 552968 | tf_op jit(solution)/shard_map/ppermute | solution.py:429
  70.0 1.6 %collective-permute-start.23 = (bf16[32,2880]{1,0:T(8,128)(2,1)S(1)}, bf16[32,2880]{1,0:T(8,128)(2,1)S(1)}, u32[]{:S(2)}, u32[]{:S(2)}) collective-permute-start(bf16[32,2880]{1,0:T(8,128)(2,1)S(1)} %shard_map.147), channel_id=1, source_target_pairs={{0,4},{1,3},{4,8},{5,1},{8,12},{9,5},{12,14},{13,9},{14,10},{15,13... | collective-permute-start | bytes 552968 | tf_op jit(solution)/shard_map/ppermute | solution.py:429
  71.7 1.6 %collective-permute-start.37 = (bf16[32,2880]{1,0:T(8,128)(2,1)S(1)}, bf16[32,2880]{1,0:T(8,128)(2,1)S(1)}, u32[]{:S(2)}, u32[]{:S(2)}) collective-permute-start(bf16[32,2880]{1,0:T(8,128)(2,1)S(1)} %shard_map.158), channel_id=1, source_target_pairs={{0,4},{1,3},{4,8},{5,1},{8,12},{9,5},{12,14},{13,9},{14,10},{15,13... | collective-permute-start | bytes 552968 | tf_op jit(solution)/shard_map/ppermute | solution.py:429
  78.4 2.0 %collective-permute-done.34.refs_3_ = bf16[32,2880]{1,0:T(8,128)(2,1)S(1)} collective-permute-done((bf16[32,2880]{1,0:T(8,128)(2,1)S(1)}, bf16[32,2880]{1,0:T(8,128)(2,1)S(1)}, u32[]{:S(2)}, u32[]{:S(2)}) %collective-permute-start.34) | collective-permute-done | bytes 184352 | tf_op jit(solution)/shard_map/ppermute | solution.py:429
  81.8 2.0 %collective-permute-done.24.refs_1_ = bf16[32,2880]{1,0:T(8,128)(2,1)S(1)} collective-permute-done((bf16[32,2880]{1,0:T(8,128)(2,1)S(1)}, bf16[32,2880]{1,0:T(8,128)(2,1)S(1)}, u32[]{:S(2)}, u32[]{:S(2)}) %collective-permute-start.24) | collective-permute-done | bytes 184352 | tf_op jit(solution)/shard_map/ppermute | solution.py:429
  (102 shorter events, 25.6 us)
Async XLA Ops:
  10.4 8.6 %collective-permute-start.3 = (bf16[64,2944]{1,0:T(8,128)(2,1)S(1)}, bf16[64,2944]{1,0:T(8,128)(2,1)S(1)}, u32[]{:S(2)}, u32[]{:S(2)}) collective-permute-start(bf16[64,2944]{1,0:T(8,128)(2,1)S(1)} %get-tuple-element.37.refs_1_), channel_id=1, source_target_pairs={{0,4},{1,3},{4,8},{5,1},{8,12},{9,5},{12,14},{13,9},{14,10},{15,13... | collective-permute-start | bytes 1130504 | tf_op jit(solution)/shard_map/ppermute | solution.py:429
  13.5 9.6 %collective-permute-start.8 = (bf16[64,2944]{1,0:T(8,128)(2,1)S(1)}, bf16[64,2944]{1,0:T(8,128)(2,1)S(1)}, u32[]{:S(2)}, u32[]{:S(2)}) collective-permute-start(bf16[64,2944]{1,0:T(8,128)(2,1)S(1)} %collective-permute-done.1.refs_2_), channel_id=1, source_target_pairs={{0,4},{1,3},{4,8},{5,1},{8,12},{9,5},{12,14},{13,9},{14,10},{15,13... | collective-permute-start | bytes 1130504 | tf_op jit(solution)/shard_map/ppermute | solution.py:429
  19.0 8.1 %collective-permute-start.6 = (bf16[64,2944]{1,0:T(8,128)(2,1)S(1)}, bf16[64,2944]{1,0:T(8,128)(2,1)S(1)}, u32[]{:S(2)}, u32[]{:S(2)}) collective-permute-start(bf16[64,2944]{1,0:T(8,128)(2,1)S(1)} %collective-permute-done.3.refs_1_), channel_id=1, source_target_pairs={{0,4},{1,3},{4,8},{5,1},{8,12},{9,5},{12,14},{13,9},{14,10},{15,13... | collective-permute-start | bytes 1130504 | tf_op jit(solution)/shard_map/ppermute | solution.py:429
  21.1 8.1 %collective-permute-start.4 = (bf16[64,2944]{1,0:T(8,128)(2,1)S(1)}, bf16[64,2944]{1,0:T(8,128)(2,1)S(1)}, u32[]{:S(2)}, u32[]{:S(2)}) collective-permute-start(bf16[64,2944]{1,0:T(8,128)(2,1)S(1)} %collective-permute-done.3.refs_1_), channel_id=1, source_target_pairs={{0,1},{1,0},{2,3},{3,2},{4,5},{5,4},{6,7},{7,6},{8,9},{9,8},{10,11... | collective-permute-start | bytes 1130504 | tf_op jit(solution)/shard_map/ppermute | solution.py:432
  23.0 9.6 %collective-permute-start.13 = (bf16[64,2944]{1,0:T(8,128)(2,1)S(1)}, bf16[64,2944]{1,0:T(8,128)(2,1)S(1)}, u32[]{:S(2)}, u32[]{:S(2)}) collective-permute-start(bf16[64,2944]{1,0:T(8,128)(2,1)S(1)} %collective-permute-done.8.refs_3_), channel_id=1, source_target_pairs={{0,4},{1,3},{4,8},{5,1},{8,12},{9,5},{12,14},{13,9},{14,10},{15,13... | collective-permute-start | bytes 1130504 | tf_op jit(solution)/shard_map/ppermute | solution.py:429
  25.1 10.0 %collective-permute-start.9 = (bf16[64,2944]{1,0:T(8,128)(2,1)S(1)}, bf16[64,2944]{1,0:T(8,128)(2,1)S(1)}, u32[]{:S(2)}, u32[]{:S(2)}) collective-permute-start(bf16[64,2944]{1,0:T(8,128)(2,1)S(1)} %collective-permute-done.8.refs_3_), channel_id=1, source_target_pairs={{0,1},{1,0},{2,3},{3,2},{4,5},{5,4},{6,7},{7,6},{8,9},{9,8},{10,11... | collective-permute-start | bytes 1130504 | tf_op jit(solution)/shard_map/ppermute | solution.py:432
  27.1 7.0 %collective-permute-start.7 = (bf16[64,2944]{1,0:T(8,128)(2,1)S(1)}, bf16[64,2944]{1,0:T(8,128)(2,1)S(1)}, u32[]{:S(2)}, u32[]{:S(2)}) collective-permute-start(bf16[64,2944]{1,0:T(8,128)(2,1)S(1)} %collective-permute-done.6.refs_1_), channel_id=1, source_target_pairs={{0,1},{1,0},{2,3},{3,2},{4,5},{5,4},{6,7},{7,6},{8,9},{9,8},{10,11... | collective-permute-start | bytes 1130504 | tf_op jit(solution)/shard_map/ppermute | solution.py:432
  27.1 8.1 %collective-permute-start.11 = (bf16[64,2944]{1,0:T(8,128)(2,1)S(1)}, bf16[64,2944]{1,0:T(8,128)(2,1)S(1)}, u32[]{:S(2)}, u32[]{:S(2)}) collective-permute-start(bf16[64,2944]{1,0:T(8,128)(2,1)S(1)} %collective-permute-done.6.refs_1_), channel_id=1, source_target_pairs={{0,4},{1,3},{4,8},{5,1},{8,12},{9,5},{12,14},{13,9},{14,10},{15,13... | collective-permute-start | bytes 1130504 | tf_op jit(solution)/shard_map/ppermute | solution.py:429
  32.4 8.9 %collective-permute-start.5 = (bf16[64,2880]{1,0:T(8,128)(2,1)S(1)}, bf16[64,2880]{1,0:T(8,128)(2,1)S(1)}, u32[]{:S(2)}, u32[]{:S(2)}) collective-permute-start(bf16[64,2880]{1,0:T(8,128)(2,1)S(1)} %get-tuple-element.42), channel_id=1, source_target_pairs={{0,1},{1,0},{2,3},{3,2},{4,5},{5,4},{6,7},{7,6},{8,9},{9,8},{10,11... | collective-permute-start | bytes 1105928 | tf_op jit(solution)/shard_map/ppermute | solution.py:432
  32.6 8.4 %collective-permute-start.18 = (bf16[64,2944]{1,0:T(8,128)(2,1)S(1)}, bf16[64,2944]{1,0:T(8,128)(2,1)S(1)}, u32[]{:S(2)}, u32[]{:S(2)}) collective-permute-start(bf16[64,2944]{1,0:T(8,128)(2,1)S(1)} %collective-permute-done.13.refs_3_), channel_id=1, source_target_pairs={{0,4},{1,3},{4,8},{5,1},{8,12},{9,5},{12,14},{13,9},{14,10},{15,13... | collective-permute-start | bytes 1130504 | tf_op jit(solution)/shard_map/ppermute | solution.py:429
  34.1 7.2 %collective-permute-start.14 = (bf16[64,2944]{1,0:T(8,128)(2,1)S(1)}, bf16[64,2944]{1,0:T(8,128)(2,1)S(1)}, u32[]{:S(2)}, u32[]{:S(2)}) collective-permute-start(bf16[64,2944]{1,0:T(8,128)(2,1)S(1)} %collective-permute-done.13.refs_3_), channel_id=1, source_target_pairs={{0,1},{1,0},{2,3},{3,2},{4,5},{5,4},{6,7},{7,6},{8,9},{9,8},{10,11... | collective-permute-start | bytes 1130504 | tf_op jit(solution)/shard_map/ppermute | solution.py:432
  35.1 6.2 %collective-permute-start.12 = (bf16[64,2944]{1,0:T(8,128)(2,1)S(1)}, bf16[64,2944]{1,0:T(8,128)(2,1)S(1)}, u32[]{:S(2)}, u32[]{:S(2)}) collective-permute-start(bf16[64,2944]{1,0:T(8,128)(2,1)S(1)} %collective-permute-done.11.refs_1_), channel_id=1, source_target_pairs={{0,1},{1,0},{2,3},{3,2},{4,5},{5,4},{6,7},{7,6},{8,9},{9,8},{10,11... | collective-permute-start | bytes 1130504 | tf_op jit(solution)/shard_map/ppermute | solution.py:432
  35.1 10.0 %collective-permute-start.16 = (bf16[64,2944]{1,0:T(8,128)(2,1)S(1)}, bf16[64,2944]{1,0:T(8,128)(2,1)S(1)}, u32[]{:S(2)}, u32[]{:S(2)}) collective-permute-start(bf16[64,2944]{1,0:T(8,128)(2,1)S(1)} %collective-permute-done.11.refs_1_), channel_id=1, source_target_pairs={{0,4},{1,3},{4,8},{5,1},{8,12},{9,5},{12,14},{13,9},{14,10},{15,13... | collective-permute-start | bytes 1130504 | tf_op jit(solution)/shard_map/ppermute | solution.py:429
  54.2 11.7 %collective-permute-start.10 = (bf16[64,2880]{1,0:T(8,128)(2,1)S(1)}, bf16[64,2880]{1,0:T(8,128)(2,1)S(1)}, u32[]{:S(2)}, u32[]{:S(2)}) collective-permute-start(bf16[64,2880]{1,0:T(8,128)(2,1)S(1)} %get-tuple-element.44), channel_id=1, source_target_pairs={{0,1},{1,0},{2,3},{3,2},{4,5},{5,4},{6,7},{7,6},{8,9},{9,8},{10,11... | collective-permute-start | bytes 1105928 | tf_op jit(solution)/shard_map/ppermute | solution.py:432
  56.0 6.3 %collective-permute-start.35 = (bf16[32,2880]{1,0:T(8,128)(2,1)S(1)}, bf16[32,2880]{1,0:T(8,128)(2,1)S(1)}, u32[]{:S(2)}, u32[]{:S(2)}) collective-permute-start(bf16[32,2880]{1,0:T(8,128)(2,1)S(1)} %shard_map.156), channel_id=1, source_target_pairs={{0,4},{1,3},{4,8},{5,1},{8,12},{9,5},{12,14},{13,9},{14,10},{15,13... | collective-permute-start | bytes 552968 | tf_op jit(solution)/shard_map/ppermute | solution.py:429
  57.6 12.4 %collective-permute-start.29 = (bf16[64,2880]{1,0:T(8,128)(2,1)S(1)}, bf16[64,2880]{1,0:T(8,128)(2,1)S(1)}, u32[]{:S(2)}, u32[]{:S(2)}) collective-permute-start(bf16[64,2880]{1,0:T(8,128)(2,1)S(1)} %get-tuple-element.54), channel_id=1, source_target_pairs={{0,1},{1,0},{2,3},{3,2},{4,5},{5,4},{6,7},{7,6},{8,9},{9,8},{10,11... | collective-permute-start | bytes 1105928 | tf_op jit(solution)/shard_map/ppermute | solution.py:432
  64.3 7.3 %collective-permute-start.36 = (bf16[32,2880]{1,0:T(8,128)(2,1)S(1)}, bf16[32,2880]{1,0:T(8,128)(2,1)S(1)}, u32[]{:S(2)}, u32[]{:S(2)}) collective-permute-start(bf16[32,2880]{1,0:T(8,128)(2,1)S(1)} %shard_map.157), channel_id=1, source_target_pairs={{0,4},{1,3},{4,8},{5,1},{8,12},{9,5},{12,14},{13,9},{14,10},{15,13... | collective-permute-start | bytes 552968 | tf_op jit(solution)/shard_map/ppermute | solution.py:429
  65.9 11.3 %collective-permute-start.2 = (bf16[64,2880]{1,0:T(8,128)(2,1)S(1)}, bf16[64,2880]{1,0:T(8,128)(2,1)S(1)}, u32[]{:S(2)}, u32[]{:S(2)}) collective-permute-start(bf16[64,2880]{1,0:T(8,128)(2,1)S(1)} %get-tuple-element.39), channel_id=1, source_target_pairs={{0,1},{1,0},{2,3},{3,2},{4,5},{5,4},{6,7},{7,6},{8,9},{9,8},{10,11... | collective-permute-start | bytes 1105928 | tf_op jit(solution)/shard_map/ppermute | solution.py:432
  66.3 6.9 %collective-permute-start.33 = (bf16[32,2880]{1,0:T(8,128)(2,1)S(1)}, bf16[32,2880]{1,0:T(8,128)(2,1)S(1)}, u32[]{:S(2)}, u32[]{:S(2)}) collective-permute-start(bf16[32,2880]{1,0:T(8,128)(2,1)S(1)} %shard_map.154), channel_id=1, source_target_pairs={{0,4},{1,3},{4,8},{5,1},{8,12},{9,5},{12,14},{13,9},{14,10},{15,13... | collective-permute-start | bytes 552968 | tf_op jit(solution)/shard_map/ppermute | solution.py:429
  70.0 6.4 %collective-permute-start.23 = (bf16[32,2880]{1,0:T(8,128)(2,1)S(1)}, bf16[32,2880]{1,0:T(8,128)(2,1)S(1)}, u32[]{:S(2)}, u32[]{:S(2)}) collective-permute-start(bf16[32,2880]{1,0:T(8,128)(2,1)S(1)} %shard_map.147), channel_id=1, source_target_pairs={{0,4},{1,3},{4,8},{5,1},{8,12},{9,5},{12,14},{13,9},{14,10},{15,13... | collective-permute-start | bytes 552968 | tf_op jit(solution)/shard_map/ppermute | solution.py:429
  71.7 6.7 %collective-permute-start.37 = (bf16[32,2880]{1,0:T(8,128)(2,1)S(1)}, bf16[32,2880]{1,0:T(8,128)(2,1)S(1)}, u32[]{:S(2)}, u32[]{:S(2)}) collective-permute-start(bf16[32,2880]{1,0:T(8,128)(2,1)S(1)} %shard_map.158), channel_id=1, source_target_pairs={{0,4},{1,3},{4,8},{5,1},{8,12},{9,5},{12,14},{13,9},{14,10},{15,13... | collective-permute-start | bytes 552968 | tf_op jit(solution)/shard_map/ppermute | solution.py:429
  73.3 7.1 %collective-permute-start.34 = (bf16[32,2880]{1,0:T(8,128)(2,1)S(1)}, bf16[32,2880]{1,0:T(8,128)(2,1)S(1)}, u32[]{:S(2)}, u32[]{:S(2)}) collective-permute-start(bf16[32,2880]{1,0:T(8,128)(2,1)S(1)} %shard_map.155), channel_id=1, source_target_pairs={{0,4},{1,3},{4,8},{5,1},{8,12},{9,5},{12,14},{13,9},{14,10},{15,13... | collective-permute-start | bytes 552968 | tf_op jit(solution)/shard_map/ppermute | solution.py:429
  74.5 7.4 %collective-permute-start.28 = (bf16[32,2880]{1,0:T(8,128)(2,1)S(1)}, bf16[32,2880]{1,0:T(8,128)(2,1)S(1)}, u32[]{:S(2)}, u32[]{:S(2)}) collective-permute-start(bf16[32,2880]{1,0:T(8,128)(2,1)S(1)} %shard_map.152), channel_id=1, source_target_pairs={{0,5},{1,2},{4,9},{5,0},{8,13},{9,4},{12,15},{13,8},{14,11},{15,12... | collective-permute-start | bytes 552968 | tf_op jit(solution)/shard_map/ppermute | solution.py:429
  76.5 7.4 %collective-permute-start.24 = (bf16[32,2880]{1,0:T(8,128)(2,1)S(1)}, bf16[32,2880]{1,0:T(8,128)(2,1)S(1)}, u32[]{:S(2)}, u32[]{:S(2)}) collective-permute-start(bf16[32,2880]{1,0:T(8,128)(2,1)S(1)} %shard_map.148), channel_id=1, source_target_pairs={{0,5},{1,2},{4,9},{5,0},{8,13},{9,4},{12,15},{13,8},{14,11},{15,12... | collective-permute-start | bytes 552968 | tf_op jit(solution)/shard_map/ppermute | solution.py:429
  (26 other events, 147.1 us)
where the time goes:
time: 84.9 us; the launch traced here: 84.7 us
  starting transfers between devices  36.6 us (43%)
  Pallas kernels  29.5 us (35%)
  waiting for transfers between devices  18.2 us (21%)
    ppermute x21, starting transfers between devices, send(): return lax.ppermute(x, ring, ring_pairs(chips, cores, cross))  33.9 us
    pallas_call x5, Pallas kernels, run_expert(): pl.pallas_call(lambda *refs: expert_kernel(count, experts, *refs), out_sh...  18 us
    ppermute x21, waiting for transfers between devices, send(): return lax.ppermute(x, ring, ring_pairs(chips, cores, cross))  16.1 us
    pallas_call x1, Pallas kernels, attend_theirs(): pl.pallas_call(first_kernel, out_shape=(jax.ShapeDtypeStruct((rows, colum...  5.48 us
    pallas_call x1, Pallas kernels, attend_mine(): pl.pallas_call(second_kernel, out_shape=jax.ShapeDtypeStruct((rows, w.sha...  3.37 us
    ppermute x17, starting transfers between devices, swap(): return lax.ppermute(x, 'exp', [(0, 1), (1, 0)])  2.68 us
    ppermute x17, waiting for transfers between devices, swap(): return lax.ppermute(x, 'exp', [(0, 1), (1, 0)])  2.08 us
  transfers between devices with their start and end apart: 38, of which 18 were waited for; matrix products, arithmetic and copies ran while one was open for 0% of the time, Pallas kernels for 22%

commit v1 on v0

--- a/solution.py
+++ b/solution.py
@@ -84,7 +84,9 @@
     return jnp.concatenate(blocks, axis=-1)
 
 
-def attend(first, lengths_ref, q_ref, nk_ref, nv_ref, k_ref, v_ref, att_ref, ready):
+def attend(
+    first, lengths_ref, q_ref, nk_ref, nv_ref, k_ref, v_ref, att_ref, keys_ready, values_ready
+):
     width = nk_ref.shape[1]
     slots = width // HEAD
     heads = q_ref.shape[1] // HEAD
@@ -96,7 +98,7 @@
     for at in batches:
         step = at // STEP * STEP
         if at == step:
-            ready(at)
+            keys_ready(at)
             queries = q_ref[step : step + STEP].astype(jnp.float32) * (1.0 / math.sqrt(HEAD))
         rows = place_heads(queries[at - step : at - step + SUB], heads, slots, width)
         keys = k_ref[at : at + SUB].reshape(SUB * cache_len, width)
@@ -110,6 +112,8 @@
     outputs = []
     for at, probs in zip(batches, turned):
         step = at // STEP * STEP
+        if at == step:
+            values_ready(at)
         values = v_ref[at : at + SUB].reshape(SUB * cache_len, width)
         outputs.append(weigh(probs, values, nv_ref[step : step + STEP], per))
     for step in range(0, att_ref.shape[0], STEP):
@@ -145,15 +149,13 @@
         bring(source.at[pl.ds(theirs, rows)], target)
         for source, target in ((q_hbm, q_ref), (nk_hbm, nk_ref), (nv_hbm, nv_ref))
     ]
-    cache = []
-    for at in range(0, rows, STEP):
-        span = pl.ds(theirs + at, STEP)
-        cache.append(
-            (
-                bring(k_hbm.at[span], k_ref.at[pl.ds(at, STEP)]),
-                bring(v_hbm.at[span], v_ref.at[pl.ds(at, STEP)]),
-            )
-        )
+    steps = range(0, rows, STEP)
+    keys = [
+        bring(k_hbm.at[pl.ds(theirs + at, STEP)], k_ref.at[pl.ds(at, STEP)]) for at in steps
+    ]
+    values = [
+        bring(v_hbm.at[pl.ds(theirs + at, STEP)], v_ref.at[pl.ds(at, STEP)]) for at in steps
+    ]
     pieces = 4
     columns = w_ref.shape[0]
     size = -(-columns // pieces // 16) * 16
@@ -168,11 +170,11 @@
     for copy in small:
         copy.wait()
 
-    def ready(at):
-        for copy in cache[at // STEP]:
-            copy.wait()
-
-    attend(theirs, lengths_ref, q_ref, nk_ref, nv_ref, k_ref, v_ref, att_ref, ready)
+    attend(
+        theirs, lengths_ref, q_ref, nk_ref, nv_ref, k_ref, v_ref, att_ref,
+        lambda at: keys[at // STEP].wait(),
+        lambda at: values[at // STEP].wait(),
+    )
     for copy in weights:
         copy.wait()
     project(att_ref, w_ref, out_ref)
@@ -186,7 +188,7 @@
     rows = out_ref.shape[0]
     mine = pl.multiple_of(core_ref[0] * rows, rows)
     own = [ref.at[pl.ds(mine, rows)] for ref in (q_ref, nk_ref, nv_ref)]
-    attend(mine, lengths_ref, *own, k_ref, v_ref, att_ref, lambda at: None)
+    attend(mine, lengths_ref, *own, k_ref, v_ref, att_ref, lambda at: None, lambda at: None)
     project(att_ref, w_ref, out_ref)
 
 
@@ -457,24 +459,21 @@
     done = expert((x, y), cost=1)
     own, own_other = done[0], swap(done[1])
     sums_x, sums_y = [None], [None]
-    swapped_y = None
     for k in range(1, far + 1):
         x = send(x)
         if k in (1, far):
             x = after(x, done[0])
         blocks = [x, swap(x)]
-        if k > 1:
-            blocks += swapped_y
         if k < far:
             y = send(y)
             if k > 1:
                 y = after(y, done[0])
             swapped_y = [y, swap(y)]
-        if 2 < k < far:
-            blocks[1] = after(blocks[1], sums_x[k - 2][1], *([sums_y[k - 2][1]] if k > 3 else []))
+        if k != far - 1:
+            blocks += swapped_y
         done = expert(blocks)
         sums_x.append((done[1], swap(done[0])))
-        if k > 1:
+        if k != far - 1:
             sums_y.append((done[3], swap(done[2])))
 
     held = add_all(hidden_state, own, own_other, dtype=jnp.float32)

time: 84.9 us -> 84.7 us (level)
  transfers between devices with their start and end apart: 38 -> 38, of which waited for: 18 -> 20; matrix products, arithmetic and copies ran while one was open for 0% -> 0% of each run, Pallas kernels for 22% -> 22%
where the time goes in v1:
time: 84.7 us; the launch traced here: 84.3 us
  starting transfers between devices  36.3 us (43%)
  Pallas kernels  29.7 us (35%)
  waiting for transfers between devices  17.9 us (21%)
    ppermute x21, starting transfers between devices, send(): return lax.ppermute(x, ring, ring_pairs(chips, cores, cross))  33.7 us
    pallas_call x5, Pallas kernels, run_expert(): pl.pallas_call(lambda *refs: expert_kernel(count, experts, *refs), out_sh...  18 us
    ppermute x21, waiting for transfers between devices, send(): return lax.ppermute(x, ring, ring_pairs(chips, cores, cross))  15.8 us
    pallas_call x1, Pallas kernels, attend_theirs(): pl.pallas_call(first_kernel, out_shape=(jax.ShapeDtypeStruct((rows, colum...  5.62 us
    pallas_call x1, Pallas kernels, attend_mine(): pl.pallas_call(second_kernel, out_shape=jax.ShapeDtypeStruct((rows, w.sha...  3.36 us
    ppermute x17, starting transfers between devices, swap(): return lax.ppermute(x, 'exp', [(0, 1), (1, 0)])  2.64 us
    ppermute x17, waiting for transfers between devices, swap(): return lax.ppermute(x, 'exp', [(0, 1), (1, 0)])  2.19 us
  transfers between devices with their start and end apart: 38, of which 20 were waited for; matrix products, arithmetic and copies ran while one was open for 0% of the time, Pallas kernels for 22%

profile of v1, /device:TPU:0, one launch (start us, length us, event | category | flops | bytes accessed | tf_op | source)
XLA Modules:
  0.0 84.3 jit_solution(18026237549881329756)
XLA Ops:
  0.0 5.6 %shard_map.136 = (f32[64,2880]{1,0:T(8,128)S(1)}, bf16[2880,1024]{1,0:T(8,128)(2,1)S(1)}, bf16[64,64,128]{2,1,0:T(8,128)(2,1)S(1)}, bf16[64,64,128]{2,1,0:T(8,128)(2,1)S(1)}) custom-call(s32[1]{0:T(128)} %bitcast.core_ref, s32[1]{0:T(128)} %bitcast.1.chip_ref.refs_0_, s32[128]{0:T(128)} %lengths_ref.1, bf16[128,1024]{1,0:T(8,128)(2,1)} %q_ref.1, ...), custom_call_target="tpu_custom_call" | custom-call | flops 377487360 | bytes 5898240 | tf_op jit(solution)/shard_map/pallas_call | solution.py:204
  6.3 3.4 %shard_map.137.mine_ref = f32[64,2880]{1,0:T(8,128)S(1)} custom-call(s32[1]{0:T(128)} %bitcast.core_ref, s32[128]{0:T(128)S(1)} %copy-done.7, bf16[128,1024]{1,0:T(8,128)(2,1)S(1)} %copy-done.2, bf16[128,128]{1,0:T(8,128)(2,1)S(1)} %copy-done.4, bf16[128,128]{1,0:T(8,128)(2,1)S(1)} %copy-done.5, bf16[64,64,128]{2,1,0:T(8,128)(2,1)S(1)} %get-tuple-element.31.k_ref, ...), custom_call_target="tpu_custom_call" | custom-call | flops 377487360 | bytes 5898240 | tf_op jit(solution)/shard_map/pallas_call | solution.py:241
  10.6 3.0 %collective-permute-start.3 = (bf16[64,2944]{1,0:T(8,128)(2,1)S(1)}, bf16[64,2944]{1,0:T(8,128)(2,1)S(1)}, u32[]{:S(2)}, u32[]{:S(2)}) collective-permute-start(bf16[64,2944]{1,0:T(8,128)(2,1)S(1)} %get-tuple-element.36.refs_1_), channel_id=1, source_target_pairs={{0,4},{1,3},{4,8},{5,1},{8,12},{9,5},{12,14},{13,9},{14,10},{15,13... | collective-permute-start | bytes 1130504 | tf_op jit(solution)/shard_map/ppermute | solution.py:431
  13.6 1.6 %collective-permute-start.5 = (bf16[64,2944]{1,0:T(8,128)(2,1)S(1)}, bf16[64,2944]{1,0:T(8,128)(2,1)S(1)}, u32[]{:S(2)}, u32[]{:S(2)}) collective-permute-start(bf16[64,2944]{1,0:T(8,128)(2,1)S(1)} %collective-permute-done.1.refs_2_), channel_id=1, source_target_pairs={{0,4},{1,3},{4,8},{5,1},{8,12},{9,5},{12,14},{13,9},{14,10},{15,13... | collective-permute-start | bytes 1130504 | tf_op jit(solution)/shard_map/ppermute | solution.py:431
  15.2 3.2 %shard_map.139 = (bf16[64,2880]{1,0:T(8,128)(2,1)S(1)}, bf16[64,2880]{1,0:T(8,128)(2,1)S(1)}) custom-call(s32[1]{0:T(128)} %bitcast.1.chip_ref.refs_0_, bf16[64,2944]{1,0:T(8,128)(2,1)S(1)} %get-tuple-element.36.refs_1_, bf16[64,2944]{1,0:T(8,128)(2,1)S(1)} %collective-permute-done.1.refs_2_, bf16[1,720,2880]{2,1,0:T(8,128)(2,1)S(1)} %bitcast.9, ...), custom_call_target="tpu_custom_call" | custom-call | flops 1592524800 | bytes 12441600 | tf_op jit(solution)/shard_map/pallas_call | solution.py:341
  19.1 2.1 %collective-permute-start.8 = (bf16[64,2944]{1,0:T(8,128)(2,1)S(1)}, bf16[64,2944]{1,0:T(8,128)(2,1)S(1)}, u32[]{:S(2)}, u32[]{:S(2)}) collective-permute-start(bf16[64,2944]{1,0:T(8,128)(2,1)S(1)} %collective-permute-done.3.refs_1_), channel_id=1, source_target_pairs={{0,4},{1,3},{4,8},{5,1},{8,12},{9,5},{12,14},{13,9},{14,10},{15,13... | collective-permute-start | bytes 1130504 | tf_op jit(solution)/shard_map/ppermute | solution.py:431
  21.2 2.0 %collective-permute-done.5.refs_3_ = bf16[64,2944]{1,0:T(8,128)(2,1)S(1)} collective-permute-done((bf16[64,2944]{1,0:T(8,128)(2,1)S(1)}, bf16[64,2944]{1,0:T(8,128)(2,1)S(1)}, u32[]{:S(2)}, u32[]{:S(2)}) %collective-permute-start.5) | collective-permute-done | bytes 376864 | tf_op jit(solution)/shard_map/ppermute | solution.py:431
  23.2 2.1 %collective-permute-start.10 = (bf16[64,2944]{1,0:T(8,128)(2,1)S(1)}, bf16[64,2944]{1,0:T(8,128)(2,1)S(1)}, u32[]{:S(2)}, u32[]{:S(2)}) collective-permute-start(bf16[64,2944]{1,0:T(8,128)(2,1)S(1)} %collective-permute-done.5.refs_3_), channel_id=1, source_target_pairs={{0,4},{1,3},{4,8},{5,1},{8,12},{9,5},{12,14},{13,9},{14,10},{15,13... | collective-permute-start | bytes 1130504 | tf_op jit(solution)/shard_map/ppermute | solution.py:431
  25.3 2.0 %collective-permute-done.8.refs_1_ = bf16[64,2944]{1,0:T(8,128)(2,1)S(1)} collective-permute-done((bf16[64,2944]{1,0:T(8,128)(2,1)S(1)}, bf16[64,2944]{1,0:T(8,128)(2,1)S(1)}, u32[]{:S(2)}, u32[]{:S(2)}) %collective-permute-start.8) | collective-permute-done | bytes 376864 | tf_op jit(solution)/shard_map/ppermute | solution.py:431
  27.2 2.1 %collective-permute-start.13 = (bf16[64,2944]{1,0:T(8,128)(2,1)S(1)}, bf16[64,2944]{1,0:T(8,128)(2,1)S(1)}, u32[]{:S(2)}, u32[]{:S(2)}) collective-permute-start(bf16[64,2944]{1,0:T(8,128)(2,1)S(1)} %collective-permute-done.8.refs_1_), channel_id=1, source_target_pairs={{0,4},{1,3},{4,8},{5,1},{8,12},{9,5},{12,14},{13,9},{14,10},{15,13... | collective-permute-start | bytes 1130504 | tf_op jit(solution)/shard_map/ppermute | solution.py:431
  29.3 3.8 %shard_map.141 = (bf16[64,2880]{1,0:T(8,128)(2,1)S(1)}, bf16[64,2880]{1,0:T(8,128)(2,1)S(1)}, bf16[64,2880]{1,0:T(8,128)(2,1)S(1)}, bf16[64,2880]{1,0:T(8,128)(2,1)S(1)}) custom-call(s32[1]{0:T(128)} %bitcast.1.chip_ref.refs_0_, bf16[64,2944]{1,0:T(8,128)(2,1)S(1)} %collective-permute-done.3.refs_1_, bf16[64,2944]{1,0:T(8,128)(2,1)S(1)} %collective-permute-done.4.refs_2_, ...), custom_call_target="tpu_custom_call" | custom-call | flops 15925248000 | bytes 62208000 | tf_op jit(solution)/shard_map/pallas_call | solution.py:341
  33.4 1.5 %collective-permute-start.18 = (bf16[64,2944]{1,0:T(8,128)(2,1)S(1)}, bf16[64,2944]{1,0:T(8,128)(2,1)S(1)}, u32[]{:S(2)}, u32[]{:S(2)}) collective-permute-start(bf16[64,2944]{1,0:T(8,128)(2,1)S(1)} %collective-permute-done.10.refs_3_), channel_id=1, source_target_pairs={{0,4},{1,3},{4,8},{5,1},{8,12},{9,5},{12,14},{13,9},{14,10},{15,13... | collective-permute-start | bytes 1130504 | tf_op jit(solution)/shard_map/ppermute | solution.py:431
  35.3 2.1 %collective-permute-start.16 = (bf16[64,2944]{1,0:T(8,128)(2,1)S(1)}, bf16[64,2944]{1,0:T(8,128)(2,1)S(1)}, u32[]{:S(2)}, u32[]{:S(2)}) collective-permute-start(bf16[64,2944]{1,0:T(8,128)(2,1)S(1)} %collective-permute-done.13.refs_1_), channel_id=1, source_target_pairs={{0,4},{1,3},{4,8},{5,1},{8,12},{9,5},{12,14},{13,9},{14,10},{15,13... | collective-permute-start | bytes 1130504 | tf_op jit(solution)/shard_map/ppermute | solution.py:431
  37.4 3.8 %shard_map.142 = (bf16[64,2880]{1,0:T(8,128)(2,1)S(1)}, bf16[64,2880]{1,0:T(8,128)(2,1)S(1)}, bf16[64,2880]{1,0:T(8,128)(2,1)S(1)}, bf16[64,2880]{1,0:T(8,128)(2,1)S(1)}) custom-call(s32[1]{0:T(128)} %bitcast.1.chip_ref.refs_0_, bf16[64,2944]{1,0:T(8,128)(2,1)S(1)} %collective-permute-done.8.refs_1_, bf16[64,2944]{1,0:T(8,128)(2,1)S(1)} %collective-permute-done.9.refs_2_, ...), custom_call_target="tpu_custom_call" | custom-call | flops 15925248000 | bytes 62208000 | tf_op jit(solution)/shard_map/pallas_call | solution.py:341
  41.5 3.2 %shard_map.143 = (bf16[64,2880]{1,0:T(8,128)(2,1)S(1)}, bf16[64,2880]{1,0:T(8,128)(2,1)S(1)}) custom-call(s32[1]{0:T(128)} %bitcast.1.chip_ref.refs_0_, bf16[64,2944]{1,0:T(8,128)(2,1)S(1)} %collective-permute-done.13.refs_1_, bf16[64,2944]{1,0:T(8,128)(2,1)S(1)} %collective-permute-done.14.refs_2_, bf16[1,720,2880]{2,1,0:T(8,128)(2,1)S(1)} %bitcast.12, ...), custom_call_target="tpu_custom_call" | custom-call | flops 7962624000 | bytes 62208000 | tf_op jit(solution)/shard_map/pallas_call | solution.py:341
  45.1 1.6 %collective-permute-done.17.refs_2_ = bf16[64,2944]{1,0:T(8,128)(2,1)S(1)} collective-permute-done((bf16[64,2944]{1,0:T(8,128)(2,1)S(1)}, bf16[64,2944]{1,0:T(8,128)(2,1)S(1)}, u32[]{:S(2)}, u32[]{:S(2)}) %collective-permute-start.17) | collective-permute-done | bytes 376864 | tf_op jit(solution)/shard_map/ppermute | solution.py:434
  46.7 3.8 %shard_map.144 = (bf16[64,2880]{1,0:T(8,128)(2,1)S(1)}, bf16[64,2880]{1,0:T(8,128)(2,1)S(1)}, bf16[64,2880]{1,0:T(8,128)(2,1)S(1)}, bf16[64,2880]{1,0:T(8,128)(2,1)S(1)}) custom-call(s32[1]{0:T(128)} %bitcast.1.chip_ref.refs_0_, bf16[64,2944]{1,0:T(8,128)(2,1)S(1)} %collective-permute-done.16.refs_1_, bf16[64,2944]{1,0:T(8,128)(2,1)S(1)} %collective-permute-done.17.refs_2_, ...), custom_call_target="tpu_custom_call" | custom-call | flops 15925248000 | bytes 62208000 | tf_op jit(solution)/shard_map/pallas_call | solution.py:341
  52.4 1.5 %collective-permute-start.25 = (bf16[32,2880]{1,0:T(8,128)(2,1)S(1)}, bf16[32,2880]{1,0:T(8,128)(2,1)S(1)}, u32[]{:S(2)}, u32[]{:S(2)}) collective-permute-start(bf16[32,2880]{1,0:T(8,128)(2,1)S(1)} %shard_map.149), channel_id=1, source_target_pairs={{0,4},{1,3},{4,8},{5,1},{8,12},{9,5},{12,14},{13,9},{14,10},{15,13... | collective-permute-start | bytes 552968 | tf_op jit(solution)/shard_map/ppermute | solution.py:431
  54.0 1.6 %collective-permute-start.21 = (bf16[32,2880]{1,0:T(8,128)(2,1)S(1)}, bf16[32,2880]{1,0:T(8,128)(2,1)S(1)}, u32[]{:S(2)}, u32[]{:S(2)}) collective-permute-start(bf16[32,2880]{1,0:T(8,128)(2,1)S(1)} %shard_map.145), channel_id=1, source_target_pairs={{0,4},{1,3},{4,8},{5,1},{8,12},{9,5},{12,14},{13,9},{14,10},{15,13... | collective-permute-start | bytes 552968 | tf_op jit(solution)/shard_map/ppermute | solution.py:431
  55.8 1.6 %collective-permute-start.35 = (bf16[32,2880]{1,0:T(8,128)(2,1)S(1)}, bf16[32,2880]{1,0:T(8,128)(2,1)S(1)}, u32[]{:S(2)}, u32[]{:S(2)}) collective-permute-start(bf16[32,2880]{1,0:T(8,128)(2,1)S(1)} %shard_map.156), channel_id=1, source_target_pairs={{0,4},{1,3},{4,8},{5,1},{8,12},{9,5},{12,14},{13,9},{14,10},{15,13... | collective-permute-start | bytes 552968 | tf_op jit(solution)/shard_map/ppermute | solution.py:431
  58.0 1.5 %collective-permute-start.32 = (bf16[32,2880]{1,0:T(8,128)(2,1)S(1)}, bf16[32,2880]{1,0:T(8,128)(2,1)S(1)}, u32[]{:S(2)}, u32[]{:S(2)}) collective-permute-start(bf16[32,2880]{1,0:T(8,128)(2,1)S(1)} %shard_map.153), channel_id=1, source_target_pairs={{0,4},{1,3},{4,8},{5,1},{8,12},{9,5},{12,14},{13,9},{14,10},{15,13... | collective-permute-start | bytes 552968 | tf_op jit(solution)/shard_map/ppermute | solution.py:431
  73.7 1.6 %collective-permute-start.34 = (bf16[32,2880]{1,0:T(8,128)(2,1)S(1)}, bf16[32,2880]{1,0:T(8,128)(2,1)S(1)}, u32[]{:S(2)}, u32[]{:S(2)}) collective-permute-start(bf16[32,2880]{1,0:T(8,128)(2,1)S(1)} %shard_map.155), channel_id=1, source_target_pairs={{0,4},{1,3},{4,8},{5,1},{8,12},{9,5},{12,14},{13,9},{14,10},{15,13... | collective-permute-start | bytes 552968 | tf_op jit(solution)/shard_map/ppermute | solution.py:431
  78.2 2.0 %collective-permute-done.34.refs_3_ = bf16[32,2880]{1,0:T(8,128)(2,1)S(1)} collective-permute-done((bf16[32,2880]{1,0:T(8,128)(2,1)S(1)}, bf16[32,2880]{1,0:T(8,128)(2,1)S(1)}, u32[]{:S(2)}, u32[]{:S(2)}) %collective-permute-start.34) | collective-permute-done | bytes 184352 | tf_op jit(solution)/shard_map/ppermute | solution.py:431
  81.4 2.0 %collective-permute-done.24.refs_1_ = bf16[32,2880]{1,0:T(8,128)(2,1)S(1)} collective-permute-done((bf16[32,2880]{1,0:T(8,128)(2,1)S(1)}, bf16[32,2880]{1,0:T(8,128)(2,1)S(1)}, u32[]{:S(2)}, u32[]{:S(2)}) %collective-permute-start.24) | collective-permute-done | bytes 184352 | tf_op jit(solution)/shard_map/ppermute | solution.py:431
  (102 shorter events, 25.2 us)
Async XLA Ops:
  10.6 8.6 %collective-permute-start.3 = (bf16[64,2944]{1,0:T(8,128)(2,1)S(1)}, bf16[64,2944]{1,0:T(8,128)(2,1)S(1)}, u32[]{:S(2)}, u32[]{:S(2)}) collective-permute-start(bf16[64,2944]{1,0:T(8,128)(2,1)S(1)} %get-tuple-element.36.refs_1_), channel_id=1, source_target_pairs={{0,4},{1,3},{4,8},{5,1},{8,12},{9,5},{12,14},{13,9},{14,10},{15,13... | collective-permute-start | bytes 1130504 | tf_op jit(solution)/shard_map/ppermute | solution.py:431
  13.6 9.6 %collective-permute-start.5 = (bf16[64,2944]{1,0:T(8,128)(2,1)S(1)}, bf16[64,2944]{1,0:T(8,128)(2,1)S(1)}, u32[]{:S(2)}, u32[]{:S(2)}) collective-permute-start(bf16[64,2944]{1,0:T(8,128)(2,1)S(1)} %collective-permute-done.1.refs_2_), channel_id=1, source_target_pairs={{0,4},{1,3},{4,8},{5,1},{8,12},{9,5},{12,14},{13,9},{14,10},{15,13... | collective-permute-start | bytes 1130504 | tf_op jit(solution)/shard_map/ppermute | solution.py:431
  19.1 8.1 %collective-permute-start.8 = (bf16[64,2944]{1,0:T(8,128)(2,1)S(1)}, bf16[64,2944]{1,0:T(8,128)(2,1)S(1)}, u32[]{:S(2)}, u32[]{:S(2)}) collective-permute-start(bf16[64,2944]{1,0:T(8,128)(2,1)S(1)} %collective-permute-done.3.refs_1_), channel_id=1, source_target_pairs={{0,4},{1,3},{4,8},{5,1},{8,12},{9,5},{12,14},{13,9},{14,10},{15,13... | collective-permute-start | bytes 1130504 | tf_op jit(solution)/shard_map/ppermute | solution.py:431
  21.2 8.1 %collective-permute-start.4 = (bf16[64,2944]{1,0:T(8,128)(2,1)S(1)}, bf16[64,2944]{1,0:T(8,128)(2,1)S(1)}, u32[]{:S(2)}, u32[]{:S(2)}) collective-permute-start(bf16[64,2944]{1,0:T(8,128)(2,1)S(1)} %collective-permute-done.3.refs_1_), channel_id=1, source_target_pairs={{0,1},{1,0},{2,3},{3,2},{4,5},{5,4},{6,7},{7,6},{8,9},{9,8},{10,11... | collective-permute-start | bytes 1130504 | tf_op jit(solution)/shard_map/ppermute | solution.py:434
  23.2 6.1 %collective-permute-start.6 = (bf16[64,2944]{1,0:T(8,128)(2,1)S(1)}, bf16[64,2944]{1,0:T(8,128)(2,1)S(1)}, u32[]{:S(2)}, u32[]{:S(2)}) collective-permute-start(bf16[64,2944]{1,0:T(8,128)(2,1)S(1)} %collective-permute-done.5.refs_3_), channel_id=1, source_target_pairs={{0,1},{1,0},{2,3},{3,2},{4,5},{5,4},{6,7},{7,6},{8,9},{9,8},{10,11... | collective-permute-start | bytes 1130504 | tf_op jit(solution)/shard_map/ppermute | solution.py:434
  23.2 10.0 %collective-permute-start.10 = (bf16[64,2944]{1,0:T(8,128)(2,1)S(1)}, bf16[64,2944]{1,0:T(8,128)(2,1)S(1)}, u32[]{:S(2)}, u32[]{:S(2)}) collective-permute-start(bf16[64,2944]{1,0:T(8,128)(2,1)S(1)} %collective-permute-done.5.refs_3_), channel_id=1, source_target_pairs={{0,4},{1,3},{4,8},{5,1},{8,12},{9,5},{12,14},{13,9},{14,10},{15,13... | collective-permute-start | bytes 1130504 | tf_op jit(solution)/shard_map/ppermute | solution.py:431
  27.2 10.2 %collective-permute-start.9 = (bf16[64,2944]{1,0:T(8,128)(2,1)S(1)}, bf16[64,2944]{1,0:T(8,128)(2,1)S(1)}, u32[]{:S(2)}, u32[]{:S(2)}) collective-permute-start(bf16[64,2944]{1,0:T(8,128)(2,1)S(1)} %collective-permute-done.8.refs_1_), channel_id=1, source_target_pairs={{0,1},{1,0},{2,3},{3,2},{4,5},{5,4},{6,7},{7,6},{8,9},{9,8},{10,11... | collective-permute-start | bytes 1130504 | tf_op jit(solution)/shard_map/ppermute | solution.py:434
  27.2 8.1 %collective-permute-start.13 = (bf16[64,2944]{1,0:T(8,128)(2,1)S(1)}, bf16[64,2944]{1,0:T(8,128)(2,1)S(1)}, u32[]{:S(2)}, u32[]{:S(2)}) collective-permute-start(bf16[64,2944]{1,0:T(8,128)(2,1)S(1)} %collective-permute-done.8.refs_1_), channel_id=1, source_target_pairs={{0,4},{1,3},{4,8},{5,1},{8,12},{9,5},{12,14},{13,9},{14,10},{15,13... | collective-permute-start | bytes 1130504 | tf_op jit(solution)/shard_map/ppermute | solution.py:431
  33.4 7.8 %collective-permute-start.18 = (bf16[64,2944]{1,0:T(8,128)(2,1)S(1)}, bf16[64,2944]{1,0:T(8,128)(2,1)S(1)}, u32[]{:S(2)}, u32[]{:S(2)}) collective-permute-start(bf16[64,2944]{1,0:T(8,128)(2,1)S(1)} %collective-permute-done.10.refs_3_), channel_id=1, source_target_pairs={{0,4},{1,3},{4,8},{5,1},{8,12},{9,5},{12,14},{13,9},{14,10},{15,13... | collective-permute-start | bytes 1130504 | tf_op jit(solution)/shard_map/ppermute | solution.py:431
  35.3 6.2 %collective-permute-start.14 = (bf16[64,2944]{1,0:T(8,128)(2,1)S(1)}, bf16[64,2944]{1,0:T(8,128)(2,1)S(1)}, u32[]{:S(2)}, u32[]{:S(2)}) collective-permute-start(bf16[64,2944]{1,0:T(8,128)(2,1)S(1)} %collective-permute-done.13.refs_1_), channel_id=1, source_target_pairs={{0,1},{1,0},{2,3},{3,2},{4,5},{5,4},{6,7},{7,6},{8,9},{9,8},{10,11... | collective-permute-start | bytes 1130504 | tf_op jit(solution)/shard_map/ppermute | solution.py:434
  35.3 9.7 %collective-permute-start.16 = (bf16[64,2944]{1,0:T(8,128)(2,1)S(1)}, bf16[64,2944]{1,0:T(8,128)(2,1)S(1)}, u32[]{:S(2)}, u32[]{:S(2)}) collective-permute-start(bf16[64,2944]{1,0:T(8,128)(2,1)S(1)} %collective-permute-done.13.refs_1_), channel_id=1, source_target_pairs={{0,4},{1,3},{4,8},{5,1},{8,12},{9,5},{12,14},{13,9},{14,10},{15,13... | collective-permute-start | bytes 1130504 | tf_op jit(solution)/shard_map/ppermute | solution.py:431
  51.7 9.9 %collective-permute-start.12 = (bf16[64,2880]{1,0:T(8,128)(2,1)S(1)}, bf16[64,2880]{1,0:T(8,128)(2,1)S(1)}, u32[]{:S(2)}, u32[]{:S(2)}) collective-permute-start(bf16[64,2880]{1,0:T(8,128)(2,1)S(1)} %get-tuple-element.44), channel_id=1, source_target_pairs={{0,1},{1,0},{2,3},{3,2},{4,5},{5,4},{6,7},{7,6},{8,9},{9,8},{10,11... | collective-permute-start | bytes 1105928 | tf_op jit(solution)/shard_map/ppermute | solution.py:434
  54.0 6.1 %collective-permute-start.21 = (bf16[32,2880]{1,0:T(8,128)(2,1)S(1)}, bf16[32,2880]{1,0:T(8,128)(2,1)S(1)}, u32[]{:S(2)}, u32[]{:S(2)}) collective-permute-start(bf16[32,2880]{1,0:T(8,128)(2,1)S(1)} %shard_map.145), channel_id=1, source_target_pairs={{0,4},{1,3},{4,8},{5,1},{8,12},{9,5},{12,14},{13,9},{14,10},{15,13... | collective-permute-start | bytes 552968 | tf_op jit(solution)/shard_map/ppermute | solution.py:431
  55.7 12.0 %collective-permute-start.29 = (bf16[64,2880]{1,0:T(8,128)(2,1)S(1)}, bf16[64,2880]{1,0:T(8,128)(2,1)S(1)}, u32[]{:S(2)}, u32[]{:S(2)}) collective-permute-start(bf16[64,2880]{1,0:T(8,128)(2,1)S(1)} %get-tuple-element.52), channel_id=1, source_target_pairs={{0,1},{1,0},{2,3},{3,2},{4,5},{5,4},{6,7},{7,6},{8,9},{9,8},{10,11... | collective-permute-start | bytes 1105928 | tf_op jit(solution)/shard_map/ppermute | solution.py:434
  55.8 6.3 %collective-permute-start.35 = (bf16[32,2880]{1,0:T(8,128)(2,1)S(1)}, bf16[32,2880]{1,0:T(8,128)(2,1)S(1)}, u32[]{:S(2)}, u32[]{:S(2)}) collective-permute-start(bf16[32,2880]{1,0:T(8,128)(2,1)S(1)} %shard_map.156), channel_id=1, source_target_pairs={{0,4},{1,3},{4,8},{5,1},{8,12},{9,5},{12,14},{13,9},{14,10},{15,13... | collective-permute-start | bytes 552968 | tf_op jit(solution)/shard_map/ppermute | solution.py:431
  58.0 6.1 %collective-permute-start.32 = (bf16[32,2880]{1,0:T(8,128)(2,1)S(1)}, bf16[32,2880]{1,0:T(8,128)(2,1)S(1)}, u32[]{:S(2)}, u32[]{:S(2)}) collective-permute-start(bf16[32,2880]{1,0:T(8,128)(2,1)S(1)} %shard_map.153), channel_id=1, source_target_pairs={{0,4},{1,3},{4,8},{5,1},{8,12},{9,5},{12,14},{13,9},{14,10},{15,13... | collective-permute-start | bytes 552968 | tf_op jit(solution)/shard_map/ppermute | solution.py:431
  60.1 6.1 %collective-permute-start.26 = (bf16[32,2880]{1,0:T(8,128)(2,1)S(1)}, bf16[32,2880]{1,0:T(8,128)(2,1)S(1)}, u32[]{:S(2)}, u32[]{:S(2)}) collective-permute-start(bf16[32,2880]{1,0:T(8,128)(2,1)S(1)} %shard_map.150), channel_id=1, source_target_pairs={{0,4},{1,3},{4,8},{5,1},{8,12},{9,5},{12,14},{13,9},{14,10},{15,13... | collective-permute-start | bytes 552968 | tf_op jit(solution)/shard_map/ppermute | solution.py:431
  61.6 12.1 %collective-permute-start.7 = (bf16[64,2880]{1,0:T(8,128)(2,1)S(1)}, bf16[64,2880]{1,0:T(8,128)(2,1)S(1)}, u32[]{:S(2)}, u32[]{:S(2)}) collective-permute-start(bf16[64,2880]{1,0:T(8,128)(2,1)S(1)} %get-tuple-element.41), channel_id=1, source_target_pairs={{0,1},{1,0},{2,3},{3,2},{4,5},{5,4},{6,7},{7,6},{8,9},{9,8},{10,11... | collective-permute-start | bytes 1105928 | tf_op jit(solution)/shard_map/ppermute | solution.py:434
  67.7 9.7 %collective-permute-start.2 = (bf16[64,2880]{1,0:T(8,128)(2,1)S(1)}, bf16[64,2880]{1,0:T(8,128)(2,1)S(1)}, u32[]{:S(2)}, u32[]{:S(2)}) collective-permute-start(bf16[64,2880]{1,0:T(8,128)(2,1)S(1)} %get-tuple-element.38), channel_id=1, source_target_pairs={{0,1},{1,0},{2,3},{3,2},{4,5},{5,4},{6,7},{7,6},{8,9},{9,8},{10,11... | collective-permute-start | bytes 1105928 | tf_op jit(solution)/shard_map/ppermute | solution.py:434
  68.1 7.2 %collective-permute-start.27 = (bf16[32,2880]{1,0:T(8,128)(2,1)S(1)}, bf16[32,2880]{1,0:T(8,128)(2,1)S(1)}, u32[]{:S(2)}, u32[]{:S(2)}) collective-permute-start(bf16[32,2880]{1,0:T(8,128)(2,1)S(1)} %shard_map.151), channel_id=1, source_target_pairs={{0,4},{1,3},{4,8},{5,1},{8,12},{9,5},{12,14},{13,9},{14,10},{15,13... | collective-permute-start | bytes 552968 | tf_op jit(solution)/shard_map/ppermute | solution.py:431
  70.2 6.1 %collective-permute-start.23 = (bf16[32,2880]{1,0:T(8,128)(2,1)S(1)}, bf16[32,2880]{1,0:T(8,128)(2,1)S(1)}, u32[]{:S(2)}, u32[]{:S(2)}) collective-permute-start(bf16[32,2880]{1,0:T(8,128)(2,1)S(1)} %shard_map.147), channel_id=1, source_target_pairs={{0,4},{1,3},{4,8},{5,1},{8,12},{9,5},{12,14},{13,9},{14,10},{15,13... | collective-permute-start | bytes 552968 | tf_op jit(solution)/shard_map/ppermute | solution.py:431
  72.2 6.1 %collective-permute-start.37 = (bf16[32,2880]{1,0:T(8,128)(2,1)S(1)}, bf16[32,2880]{1,0:T(8,128)(2,1)S(1)}, u32[]{:S(2)}, u32[]{:S(2)}) collective-permute-start(bf16[32,2880]{1,0:T(8,128)(2,1)S(1)} %shard_map.158), channel_id=1, source_target_pairs={{0,4},{1,3},{4,8},{5,1},{8,12},{9,5},{12,14},{13,9},{14,10},{15,13... | collective-permute-start | bytes 552968 | tf_op jit(solution)/shard_map/ppermute | solution.py:431
  73.7 6.5 %collective-permute-start.34 = (bf16[32,2880]{1,0:T(8,128)(2,1)S(1)}, bf16[32,2880]{1,0:T(8,128)(2,1)S(1)}, u32[]{:S(2)}, u32[]{:S(2)}) collective-permute-start(bf16[32,2880]{1,0:T(8,128)(2,1)S(1)} %shard_map.155), channel_id=1, source_target_pairs={{0,4},{1,3},{4,8},{5,1},{8,12},{9,5},{12,14},{13,9},{14,10},{15,13... | collective-permute-start | bytes 552968 | tf_op jit(solution)/shard_map/ppermute | solution.py:431
  76.3 7.2 %collective-permute-start.24 = (bf16[32,2880]{1,0:T(8,128)(2,1)S(1)}, bf16[32,2880]{1,0:T(8,128)(2,1)S(1)}, u32[]{:S(2)}, u32[]{:S(2)}) collective-permute-start(bf16[32,2880]{1,0:T(8,128)(2,1)S(1)} %shard_map.148), channel_id=1, source_target_pairs={{0,5},{1,2},{4,9},{5,0},{8,13},{9,4},{12,15},{13,8},{14,11},{15,12... | collective-permute-start | bytes 552968 | tf_op jit(solution)/shard_map/ppermute | solution.py:431
  (26 other events, 144.1 us)
